TPU v7x, 512 devices: a whole 4x4x16 slice. The times are simulated.
512 devices in a mesh: grp: 16 (over x, y), dev: 32 (over z, core).
Axes of the slice: x: 4, y: 4, z: 16, core: 2. Of those that a mesh axis runs over, the one named last changes fastest.
Arguments:
- records: bfloat16 [131072, 128], P('grp', 'dev')
- dropout: int32 [131072, 128], P('grp', 'dev'), may hold values 0 or 1
- counts: int32 [512], P(('grp', 'dev')), may hold values from 128 to 256, as said below
Outputs:
- upper: float32 [512, 512], replicated
- basis: bfloat16 [131072, 512], P(('grp', 'dev'))
Inputs may be any that keep to these rules, and one draw needn't show every extreme that they name: `counts`: at least one time shard has all 256 rows valid.
All inputs are finite; a program needn't handle non-finite values. No bound on the sum of `dropout` on one device may be relied on, other than what follows from the above.
Results may differ from a plain program's by a relative error of at most 0.0012.
Values may be sent and summed in bfloat16 or wider, within the bound.
No kernel may reach another device: no remote copies, remote signals or barrier semaphores. Data moves between devices by JAX's collectives and lax.ppermute only.
A program may use at most 128 MiB of HBM per device.

v0:
```python
import jax
import jax.numpy as jnp
from jax import lax
from jax.sharding import PartitionSpec as P

LAGS = 4


def from_behind(value, axis, by):
    size = lax.axis_size(axis)
    pairs = [(i, i + by) for i in range(size) if 0 <= i + by < size]
    return lax.ppermute(value, axis, pairs)


def gram_term(piece):
    return lax.dot_general(
        piece, piece, (((0,), (0,)), ((), ())), preferred_element_type=jnp.float32
    )


def project(piece, high, low):
    first = jnp.dot(piece, high, preferred_element_type=jnp.float32)
    second = jnp.dot(piece, low, preferred_element_type=jnp.float32)
    return (first + second).astype(jnp.bfloat16)


def exact_dot(left, right):
    return jnp.dot(left, right, precision=lax.Precision.HIGHEST)


def factor_block(block):
    size = block.shape[0]
    augmented = jnp.concatenate([block, jnp.eye(size, dtype=jnp.float32)], axis=1)
    order = jnp.arange(size, dtype=jnp.int32)

    def eliminate(step, state):
        working, written = state
        pivot_row = lax.dynamic_slice_in_dim(working, step, 1, 0)[0]
        pivot = lax.dynamic_slice_in_dim(pivot_row, step, 1, 0)[0]
        scaled = pivot_row / jnp.sqrt(pivot)
        column = lax.dynamic_slice_in_dim(working, step, 1, 1)[:, 0]
        factor = jnp.where(order > step, column / pivot, jnp.zeros_like(column))
        working = working - factor[:, None] * pivot_row[None, :]
        written = lax.dynamic_update_slice_in_dim(written, scaled[None, :], step, 0)
        return (working, written)

    _, written = lax.fori_loop(0, size, eliminate, (augmented, jnp.zeros_like(augmented)))
    upper_block = jnp.triu(written[:, :size])
    lower_inverse = jnp.tril(written[:, size:])
    return (upper_block, lower_inverse)


def factor_parts(matrix):
    size = matrix.shape[0]
    panel = min(128, size)
    panels = size // panel
    working = matrix
    diag_blocks = []
    diag_inverses = []
    right_blocks = []
    for number in range(panels):
        upper_block, lower_inverse = factor_block(working[:panel, :panel])
        beside = exact_dot(lower_inverse, working[:panel, panel:])
        working = working[panel:, panel:] - exact_dot(jnp.transpose(beside), beside)
        diag_blocks.append(upper_block)
        diag_inverses.append(jnp.transpose(lower_inverse))
        right_blocks.append(beside)
    block_rows = []
    for number in range(panels):
        pieces = []
        if number > 0:
            pieces.append(jnp.zeros((panel, number * panel), jnp.float32))
        pieces.append(diag_blocks[number])
        if number + 1 < panels:
            pieces.append(right_blocks[number])
        block_rows.append(jnp.concatenate(pieces, axis=1))
    upper = jnp.concatenate(block_rows, axis=0)
    solved = [[None] * panels for number in range(panels)]
    for column in range(panels):
        solved[column][column] = diag_inverses[column]
        for row in range(column - 1, -1, -1):
            accum = jnp.zeros((panel, panel), jnp.float32)
            for middle in range(row + 1, column + 1):
                coupling = upper[
                    row * panel : (row + 1) * panel, middle * panel : (middle + 1) * panel
                ]
                accum = accum + exact_dot(coupling, solved[middle][column])
            solved[row][column] = -exact_dot(diag_inverses[row], accum)
    inverse_rows = []
    for row in range(panels):
        pieces = []
        for column in range(panels):
            if column < row:
                pieces.append(jnp.zeros((panel, panel), jnp.float32))
            else:
                pieces.append(solved[row][column])
        inverse_rows.append(jnp.concatenate(pieces, axis=1))
    return (upper, jnp.concatenate(inverse_rows, axis=0))


def shards(records, dropout, counts):
    local = (records.astype(jnp.float32) * dropout.astype(jnp.float32)).astype(jnp.bfloat16)
    series = lax.all_to_all(local, "dev", split_axis=0, concat_axis=1, tiled=True)
    rows = series.shape[0]
    ahead = from_behind(series[: LAGS - 1], ("grp", "dev"), -1)
    padded = jnp.concatenate([series, ahead], axis=0)
    hankel = jnp.concatenate([padded[k : k + rows] for k in range(LAGS)], axis=1)
    valid = jnp.arange(rows, dtype=jnp.int32) >= rows - counts[0]
    hankel = jnp.where(valid[:, None], hankel, jnp.zeros_like(hankel))
    total_rows = rows * lax.axis_size("grp") * lax.axis_size("dev")
    partial_value = gram_term(hankel)
    gram = lax.psum(partial_value, ("grp", "dev"))
    upper, inverse = factor_parts(gram / total_rows)
    high = inverse.astype(jnp.bfloat16)
    low = (inverse - lax.optimization_barrier(high).astype(jnp.float32)).astype(jnp.bfloat16)
    basis = project(hankel, high, low)
    return (upper, basis)


def solution(mesh):
    in_specs = (P("grp", "dev"), P("grp", "dev"), P(("grp", "dev")))
    out_specs = (P(), P(("grp", "dev"), None))
    return jax.shard_map(shards, mesh=mesh, in_specs=in_specs, out_specs=out_specs, check_vma=False)
```

profile of v0, /device:TPU:1, one launch (start us, length us, event | category | flops | bytes accessed | tf_op | source)
XLA Modules:
  0.0 1999.9 jit_solution(4296532873974421739)
XLA Ops:
  7.2 1.6 multiply_convert_fusion
  8.7 16.8 all-to-all-start
  26.2 12.4 all-to-all-done
  38.6 3.5 collective-permute-start
  42.1 1.7 collective-permute-done
  44.0 1.3 fusion.66
  45.4 462.2 %all-reduce.3.cloned.1.call-done = f32[512,512]{1,0:T(8,128)} async-done(((f32[512,512]{1,0:T(8,128)}), f32[512,512]{1,0:T(8,128)}) %all-reduce.3.cloned.1.call-update) | async-done | bytes 1048592 | tf_op jit(solution)/shard_map/psum | solution.py:112
  507.6 1.3 broadcast_multiply_fusion
  509.1 368.6 %while.76 = (s32[]{:T(128)}, f32[128,256]{0,1:T(8,128)S(1)}, f32[128,256]{0,1:T(8,128)S(1)}, s32[]{:T(128)}, s32[]{:T(128)}, /*index=5*/s32[]{:T(128)}, s32[]{:T(128)}) while((s32[]{:T(128)}, f32[128,256]{0,1:T(8,128)S(1)}, f32[128,256]{0,1:T(8,128)S(1)}, s32[]{:T(128)}, s32[]{:T(128)}, /*index=5*/s32[]{:T(128)}, s32[]{:T(128)}) %tuple.188), condition=%wide.region_2.3_spmd.clone, body=%wide.region_1.2_spmd.clone.sunk | while | flops 66180 | bytes 271501 | solution.py:47
  513.9 0.7 fusion.92
  522.6 0.7 fusion.92
  531.2 0.7 fusion.92
  539.8 0.7 fusion.92
  542.7 0.7 fusion.92
  548.5 0.7 fusion.92
  551.4 0.7 fusion.92
  560.0 0.7 fusion.92
  568.7 0.7 fusion.92
  577.3 0.7 fusion.92
  585.9 0.7 fusion.92
  594.6 0.7 fusion.92
  597.5 0.7 fusion.92
  603.2 0.7 fusion.92
  606.1 0.7 fusion.92
  614.7 0.7 fusion.92
  623.4 0.7 fusion.92
  632.0 0.7 fusion.92
  640.7 0.7 fusion.92
  649.3 0.7 fusion.92
  652.2 0.7 fusion.92
  657.9 0.7 fusion.92
  660.8 0.7 fusion.92
  669.5 0.7 fusion.92
  678.1 0.7 fusion.92
  686.8 0.7 fusion.92
  695.4 0.7 fusion.92
  704.0 0.7 fusion.92
  706.9 0.7 fusion.92
  712.7 0.7 fusion.92
  715.6 0.7 fusion.92
  724.2 0.7 fusion.92
  732.8 0.7 fusion.92
  878.0 0.7 convolution_subtract_fusion
  878.9 368.6 %while.77 = (s32[]{:T(128)}, f32[128,256]{0,1:T(8,128)S(1)}, f32[128,256]{0,1:T(8,128)S(1)}, s32[]{:T(128)}, s32[]{:T(128)}, /*index=5*/s32[]{:T(128)}, s32[]{:T(128)}) while((s32[]{:T(128)}, f32[128,256]{0,1:T(8,128)S(1)}, f32[128,256]{0,1:T(8,128)S(1)}, s32[]{:T(128)}, s32[]{:T(128)}, /*index=5*/s32[]{:T(128)}, s32[]{:T(128)}) %tuple.191), condition=%wide.region_4.5_spmd.clone, body=%wide.region_3.4_spmd.clone.sunk | while | flops 66180 | bytes 271501 | solution.py:47
  1248.6 368.6 %while.78 = (s32[]{:T(128)}, f32[128,256]{0,1:T(8,128)S(1)}, f32[128,256]{0,1:T(8,128)S(1)}, s32[]{:T(128)}, s32[]{:T(128)}, /*index=5*/s32[]{:T(128)}, s32[]{:T(128)}) while((s32[]{:T(128)}, f32[128,256]{0,1:T(8,128)S(1)}, f32[128,256]{0,1:T(8,128)S(1)}, s32[]{:T(128)}, s32[]{:T(128)}, /*index=5*/s32[]{:T(128)}, s32[]{:T(128)}) %tuple.194), condition=%wide.region_6.7_spmd.clone, body=%wide.region_5.6_spmd.clone.sunk | while | flops 66180 | bytes 271501 | solution.py:47
  1618.2 368.6 %while.79 = (s32[]{:T(128)}, f32[128,256]{0,1:T(8,128)S(1)}, f32[128,256]{0,1:T(8,128)S(1)}, s32[]{:T(128)}, s32[]{:T(128)}, /*index=5*/s32[]{:T(128)}, s32[]{:T(128)}) while((s32[]{:T(128)}, f32[128,256]{0,1:T(8,128)S(1)}, f32[128,256]{0,1:T(8,128)S(1)}, s32[]{:T(128)}, s32[]{:T(128)}, /*index=5*/s32[]{:T(128)}, s32[]{:T(128)}) %tuple.197), condition=%wide.region_8.9_spmd.clone, body=%wide.region_7.8_spmd.clone.sunk | while | flops 66180 | bytes 271501 | solution.py:47
  1990.8 1.1 fusion.12
  1992.0 1.1 fusion.16
  (2585 shorter events, 1082.8 us)
Async XLA Ops:
  8.7 29.8 %all-to-all-start = ((bf16[32,256,4]{1,2,0:T(4,128)(2,1)}), bf16[32,256,4]{1,2,0:T(4,128)(2,1)S(1)}, u32[]{:S(2)}, u32[]{:S(2)}) async-start(bf16[32,256,4]{1,2,0:T(4,128)(2,1)} %bitcast.1), calls=%async_computation | async-start | bytes 131072 | tf_op jit(solution)/shard_map/all_to_all | solution.py:103
  25.5 482.1 %all-reduce.3.cloned.1.call-start = ((), (), s32[]{:S(2)}) async-start(), calls=%async_computation.1 | async-start | bytes 2097152 | tf_op jit(solution)/shard_map/psum | solution.py:112
  38.6 5.2 collective-permute-start
Sparse Core Ops, SparseCore 0:
  45.4 462.1 all-reduce.2
where the time goes:
time: 2020 us; the launch traced here: 2000 us
  local copies, waits for them, and re-layouts  614 us (30%)
  other arithmetic  489 us (24%)
  waiting for transfers between devices  476 us (24%)
  loops' own time  377 us (19%)
  starting transfers between devices  20.3 us (1%)
    psum x1, waiting for transfers between devices, shards(): gram = lax.psum(partial_value, ('grp', 'dev'))  462 us
    another operation x4, loops' own time, factor_block(): lax.fori_loop(0, size, eliminate, (augmented, jnp.zeros_like(augmented)))  377 us
    mul x512, other arithmetic, eliminate(): working = working - factor[:, None] * pivot_row[None, :]  337 us
    dynamic_update_slice x512, local copies, waits for them, and re-layouts, eliminate(): written = lax.dynamic_update_slice_in_dim(written, scaled[None, :], step, 0)  312 us
    dynamic_slice x512, local copies, waits for them, and re-layouts, eliminate(): pivot = lax.dynamic_slice_in_dim(pivot_row, step, 1, 0)[0]  301 us
    div x512, other arithmetic, eliminate(): scaled = pivot_row / jnp.sqrt(pivot)  94.6 us
    sub x512, other arithmetic, eliminate(): working = working - factor[:, None] * pivot_row[None, :]  53.9 us
  transfers between devices with their start and end apart: 3, of which 3 were waited for; matrix products, arithmetic and copies ran while one was open for 0% of the time, Pallas kernels for 0%

commit v1 on v0

--- a/solution.py
+++ b/solution.py
@@ -109,7 +109,8 @@
     hankel = jnp.where(valid[:, None], hankel, jnp.zeros_like(hankel))
     total_rows = rows * lax.axis_size("grp") * lax.axis_size("dev")
     partial_value = gram_term(hankel)
-    gram = lax.psum(partial_value, ("grp", "dev"))
+    one_axis = lax.psum(partial_value, "grp")
+    gram = lax.psum(one_axis, "dev")
     upper, inverse = factor_parts(gram / total_rows)
     high = inverse.astype(jnp.bfloat16)
     low = (inverse - lax.optimization_barrier(high).astype(jnp.float32)).astype(jnp.bfloat16)

time: 2020 us -> 1870 us (0.926)
  waiting for transfers between devices: 476 us -> 339 us
    psum x1 -> x2, waiting for transfers between devices: 462 us -> 325 us  [the longest x1 213 us: shards(): gram = lax.psum(one_axis, 'dev')]
  transfers between devices with their start and end apart: 3 -> 4, of which waited for: 3 -> 4; matrix products, arithmetic and copies ran while one was open for 0% -> 0% of each run, Pallas kernels for 0% -> 0%
where the time goes in v1:
time: 1870 us; the launch traced here: 1860 us
  local copies, waits for them, and re-layouts  618 us (33%)
  other arithmetic  484 us (26%)
  loops' own time  372 us (20%)
  waiting for transfers between devices  339 us (18%)
  starting transfers between devices  20.3 us (1%)
    another operation x4, loops' own time, factor_block(): lax.fori_loop(0, size, eliminate, (augmented, jnp.zeros_like(augmented)))  372 us
    mul x512, other arithmetic, eliminate(): working = working - factor[:, None] * pivot_row[None, :]  331 us
    dynamic_update_slice x512, local copies, waits for them, and re-layouts, eliminate(): written = lax.dynamic_update_slice_in_dim(written, scaled[None, :], step, 0)  312 us
    dynamic_slice x512, local copies, waits for them, and re-layouts, eliminate(): pivot = lax.dynamic_slice_in_dim(pivot_row, step, 1, 0)[0]  305 us
    psum x1, waiting for transfers between devices, shards(): gram = lax.psum(one_axis, 'dev')  213 us
    psum x1, waiting for transfers between devices, shards(): one_axis = lax.psum(partial_value, 'grp')  111 us
    div x512, other arithmetic, eliminate(): scaled = pivot_row / jnp.sqrt(pivot)  94.6 us
    sub x512, other arithmetic, eliminate(): working = working - factor[:, None] * pivot_row[None, :]  53.9 us
  transfers between devices with their start and end apart: 4, of which 4 were waited for; matrix products, arithmetic and copies ran while one was open for 0% of the time, Pallas kernels for 0%

profile of v1, /device:TPU:1, one launch (start us, length us, event | category | flops | bytes accessed | tf_op | source)
XLA Modules:
  0.0 1856.3 jit_solution(7203295625269396698)
XLA Ops:
  7.2 1.6 multiply_convert_fusion
  8.7 16.8 all-to-all-start
  26.2 12.4 all-to-all-done
  38.6 3.5 collective-permute-start
  42.1 1.7 collective-permute-done
  44.0 1.3 fusion.66
  45.4 111.4 %all-reduce.4.cloned.1.call-done = f32[512,512]{1,0:T(8,128)} async-done(((f32[512,512]{1,0:T(8,128)}), f32[512,512]{1,0:T(8,128)}) %all-reduce.4.cloned.1.call-update) | async-done | bytes 1048592 | tf_op jit(solution)/shard_map/psum | solution.py:112
  156.8 213.3 %all-reduce.6.cloned.1.call-done = f32[512,512]{1,0:T(8,128)} async-done(((f32[512,512]{1,0:T(8,128)}), f32[512,512]{1,0:T(8,128)}) %all-reduce.6.cloned.1.call-update) | async-done | bytes 1048592 | tf_op jit(solution)/shard_map/psum | solution.py:113
  370.1 1.3 broadcast_multiply_fusion
  371.6 362.4 %while.76 = (s32[]{:T(128)}, f32[128,256]{0,1:T(8,128)S(1)}, f32[128,256]{0,1:T(8,128)S(1)}, s32[]{:T(128)}, s32[]{:T(128)}, /*index=5*/s32[]{:T(128)}, s32[]{:T(128)}) while((s32[]{:T(128)}, f32[128,256]{0,1:T(8,128)S(1)}, f32[128,256]{0,1:T(8,128)S(1)}, s32[]{:T(128)}, s32[]{:T(128)}, /*index=5*/s32[]{:T(128)}, s32[]{:T(128)}) %tuple.188), condition=%wide.region_3.4_spmd.clone, body=%wide.region_2.3_spmd.clone.sunk | while | flops 66180 | bytes 271501 | solution.py:47
  734.4 0.7 convolution_subtract_fusion
  735.2 368.6 %while.77 = (s32[]{:T(128)}, f32[128,256]{0,1:T(8,128)S(1)}, f32[128,256]{0,1:T(8,128)S(1)}, s32[]{:T(128)}, s32[]{:T(128)}, /*index=5*/s32[]{:T(128)}, s32[]{:T(128)}) while((s32[]{:T(128)}, f32[128,256]{0,1:T(8,128)S(1)}, f32[128,256]{0,1:T(8,128)S(1)}, s32[]{:T(128)}, s32[]{:T(128)}, /*index=5*/s32[]{:T(128)}, s32[]{:T(128)}) %tuple.191), condition=%wide.region_5.6_spmd.clone, body=%wide.region_4.5_spmd.clone.sunk | while | flops 66180 | bytes 271501 | solution.py:47
  737.2 0.7 fusion.93
  745.9 0.7 fusion.93
  751.6 0.7 fusion.93
  754.5 0.7 fusion.93
  760.3 0.7 fusion.93
  768.9 0.7 fusion.93
  777.6 0.7 fusion.93
  783.3 0.7 fusion.93
  792.0 0.7 fusion.93
  800.6 0.7 fusion.93
  806.4 0.7 fusion.93
  809.2 0.7 fusion.93
  815.0 0.7 fusion.93
  823.7 0.7 fusion.93
  832.3 0.7 fusion.93
  838.1 0.7 fusion.93
  846.7 0.7 fusion.93
  855.3 0.7 fusion.93
  861.1 0.7 fusion.93
  864.0 0.7 fusion.93
  869.7 0.7 fusion.93
  878.4 0.7 fusion.93
  887.0 0.7 fusion.93
  892.8 0.7 fusion.93
  901.4 0.7 fusion.93
  910.1 0.7 fusion.93
  915.8 0.7 fusion.93
  918.7 0.7 fusion.93
  924.5 0.7 fusion.93
  933.1 0.7 fusion.93
  941.8 0.7 fusion.93
  947.5 0.7 fusion.93
  1105.0 368.6 %while.78 = (s32[]{:T(128)}, f32[128,256]{0,1:T(8,128)S(1)}, f32[128,256]{0,1:T(8,128)S(1)}, s32[]{:T(128)}, s32[]{:T(128)}, /*index=5*/s32[]{:T(128)}, s32[]{:T(128)}) while((s32[]{:T(128)}, f32[128,256]{0,1:T(8,128)S(1)}, f32[128,256]{0,1:T(8,128)S(1)}, s32[]{:T(128)}, s32[]{:T(128)}, /*index=5*/s32[]{:T(128)}, s32[]{:T(128)}) %tuple.194), condition=%wide.region_7.8_spmd.clone, body=%wide.region_6.7_spmd.clone.sunk | while | flops 66180 | bytes 271501 | solution.py:47
  1474.6 368.6 %while.79 = (s32[]{:T(128)}, f32[128,256]{0,1:T(8,128)S(1)}, f32[128,256]{0,1:T(8,128)S(1)}, s32[]{:T(128)}, s32[]{:T(128)}, /*index=5*/s32[]{:T(128)}, s32[]{:T(128)}) while((s32[]{:T(128)}, f32[128,256]{0,1:T(8,128)S(1)}, f32[128,256]{0,1:T(8,128)S(1)}, s32[]{:T(128)}, s32[]{:T(128)}, /*index=5*/s32[]{:T(128)}, s32[]{:T(128)}) %tuple.197), condition=%wide.region_9.10_spmd.clone, body=%wide.region_8.9_spmd.clone.sunk | while | flops 66180 | bytes 271501 | solution.py:47
  1847.2 1.1 fusion.12
  1848.4 1.1 fusion.16
  (2588 shorter events, 1082.3 us)
Async XLA Ops:
  8.7 29.8 %all-to-all-start = ((bf16[32,256,4]{1,2,0:T(4,128)(2,1)}), bf16[32,256,4]{1,2,0:T(4,128)(2,1)S(1)}, u32[]{:S(2)}, u32[]{:S(2)}) async-start(bf16[32,256,4]{1,2,0:T(4,128)(2,1)} %bitcast.1), calls=%async_computation | async-start | bytes 131072 | tf_op jit(solution)/shard_map/all_to_all | solution.py:103
  25.5 131.3 %all-reduce.4.cloned.1.call-start = ((), (), s32[]{:S(2)}) async-start(), calls=%async_computation.1 | async-start | bytes 2097152 | tf_op jit(solution)/shard_map/psum | solution.py:112
  38.6 5.2 collective-permute-start
  45.3 324.8 %all-reduce.6.cloned.1.call-start = ((), (), s32[]{:S(2)}) async-start(), calls=%async_computation.2 | async-start | bytes 2097152 | tf_op jit(solution)/shard_map/psum | solution.py:113
Sparse Core Ops, SparseCore 0:
  45.4 111.2 all-reduce.3
  159.1 210.9 all-reduce.5
